TPU v7x, 128 devices: a whole 4x4x4 slice. The times are simulated.
128 devices in a mesh: grp: 8 (over x_lo, y), ctx: 16 (over z, x_hi, core).
Axes of the slice: x: 4 (x_hi: 2, x_lo: 2; x = x_hi * 2 + x_lo), y: 4, z: 4, core: 2. Of those that a mesh axis runs over, the one named last changes fastest.
Arguments:
- tokens: bfloat16 [8, 2048, 1024], P('grp', 'ctx'), may hold values from -6 to 6
- blocks: int32 [8, 2048], P('grp'), may hold values from 0 to 15, never falling along the last dimension, each value on 1 to 256 neighbouring positions
- w_query: bfloat16 [1024, 1024], P(('grp', 'ctx')), may hold values from -0.1875 to 0.1875
- w_key: bfloat16 [1024, 1024], P(('grp', 'ctx')), may hold values from -0.1875 to 0.1875
- w_value: bfloat16 [1024, 1024], P(('grp', 'ctx')), may hold values from -0.1875 to 0.1875
- w_out: bfloat16 [1024, 1024], P(('grp', 'ctx')), may hold values from -1 to 1
- w_gate: bfloat16 [1024, 2816], P(('grp', 'ctx')), may hold values from -0.1875 to 0.1875
- w_up: bfloat16 [1024, 2816], P(('grp', 'ctx')), may hold values from -0.1875 to 0.1875
- w_down: bfloat16 [2816, 1024], P(None, ('grp', 'ctx')), may hold values from -0.109375 to 0.109375
- norm_attn: bfloat16 [1024], P(('grp', 'ctx')), may hold values from 0.099609375 to 1.8984375
- norm_mlp: bfloat16 [1024], P(('grp', 'ctx')), may hold values from 0.099609375 to 1.8984375
- cotangent: bfloat16 [8, 2048, 1024], P('grp', 'ctx'), may hold values from -6 to 6
Outputs:
- output: bfloat16 [8, 2048, 1024], P('grp', 'ctx')
- grad_tokens: float32 [8, 2048, 1024], P('grp', 'ctx')
- grad_query: float32 [1024, 1024], P('ctx')
- grad_key: float32 [1024, 1024], P('ctx')
- grad_value: float32 [1024, 1024], P('ctx')
- grad_out: float32 [1024, 1024], P('ctx')
- grad_gate: float32 [1024, 2816], P('ctx')
- grad_up: float32 [1024, 2816], P('ctx')
- grad_down: float32 [2816, 1024], P(None, 'ctx')
- grad_norm_attn: float32 [1024], P('ctx')
- grad_norm_mlp: float32 [1024], P('ctx')
Inputs may be any that keep to these rules, and one draw needn't show every extreme that they name: `blocks`: along each sequence the ids never fall; each id covers 1 to 256 consecutive tokens, and some id covers exactly 256.
All inputs are finite; a program needn't handle non-finite values.
Results may differ from a plain program's by a relative error of at most 0.025.
Values may be sent and summed in bfloat16 or wider, within the bound.
A program may use at most 256 MiB of HBM per device.

v0:
```python
import functools
import types

import jax
import jax.numpy as jnp
import numpy as np
from jax import lax
from jax.experimental import pallas as pl
from jax.experimental.pallas import tpu as pltpu
from jax.sharding import PartitionSpec as P

MESH = pl.DeviceIdType.MESH
F32 = jnp.float32
BF16 = jnp.bfloat16
EPS = 1e-05
HD = 64
SLICE = 352
WIDE = 384
QKV, GATE, DOWN, OUT = 0, 384, 1152, 1536
NEAR = (0, 1, 3, 2)


def mm(left, right):
    return jnp.dot(left, right, preferred_element_type=F32)


def mt(left, right):
    return lax.dot_general(left, right, (((1,), (1,)), ((), ())), preferred_element_type=F32)


def tm(left, right):
    return lax.dot_general(left, right, (((0,), (0,)), ((), ())), preferred_element_type=F32)


def window(s):
    rest = s * SLICE % 128
    return s * SLICE - rest, WIDE if rest + SLICE <= WIDE else WIDE + 128, rest


def turn(values, cosine, sine):
    lane = lax.broadcasted_iota(jnp.int32, values.shape, 1)
    ahead = pltpu.roll(values, 96, 1)
    behind = pltpu.roll(values, 32, 1)
    return values * cosine + jnp.where(lax.rem(lane, 64) < 32, ahead, behind) * sine


HELD = dict(
    wsrc=((2, 8, 6656), F32),
    ff=((8, 4, 16, 1152), BF16),
    fq=((8, 64, 512), BF16),
    sq=((64, 512), BF16),
    sf=((4, 16, 1152), BF16),
    zf=((4, 16, 1152), BF16),
    fo=((8, 64, 128), BF16),
    relay=((4, 16, 1152), BF16),
    pair=((16, 6656), F32),
    wz=((4, 16, 2048), BF16),
    wrow=((4, 16, 2048), BF16),
    w=((2, 4, 4, 2, 16, 1536), BF16),
    wo=((2, 2, 4, 4, 2, 16, 512), BF16),
    u1=((4, 2, 128, 1024), BF16),
    gg=((4, 2, 128, 1024), BF16),
    u2=((4, 2, 128, 1024), BF16),
    db=((4, 2, 128, 1024), BF16),
    cos=((4, 256, 128), F32),
    sin=((4, 256, 128), F32),
    q=((4, 256, 128), BF16),
    kv=((4, 2, 2, 256, 128), BF16),
    score=((2, 4, 256, 512), F32),
    kt=((4, 128, 512), BF16),
    u1t=((1024, 1024), BF16),
    dkv=((4, 2, 256, 256), F32),
    top=((2, 256, 128), F32),
    acc=((2, 256, 128), F32),
    mix=((4, 256, 128), F32),
    mixb=((4, 2, 128, 128), BF16),
    mixin=((4, 2, 128, 128), BF16),
    lse=((4, 256, 128), F32),
    hidden=((128, 1024), F32),
    unit2=((128, 1024), F32),
    r2=((128, 1), F32),
    dgu=((4, 256, 2 * WIDE), BF16),
    act=((16, 64, WIDE), BF16),
    gh=((128, 1024), F32),
    dmixb=((4, 2, 128, 128), BF16),
    dmix=((4, 2, 128, 128), BF16),
    dq=((4, 256, 128), F32),
    dqt=((128, 256), F32),
    dkvs=((4, 2, 256, 128), BF16),
    dkvr=((4, 2, 256, 128), BF16),
    dqkv=((4, 256, 384), BF16),
    go=((2, 8, 64, 128), BF16),
    gor=((15, 64, 128), BF16),
    so=((64, 128), BF16),
)
for kind in ("e2", "out", "e1"):
    HELD[kind + "p"] = ((4, 2, 128, 1024), BF16)
    HELD[kind + "d"] = ((4, 128, 1024), BF16)
    HELD[kind + "r"] = ((3, 128, 1024), BF16)
SPLIT = {"f": (512, 640), "q": (256, 128)}
ROWS = {"f": (4, 4, 4, 16), "q": (4, 4, 64)}
for kind, (by_x, by_y) in SPLIT.items():
    HELD["g" + kind] = (ROWS[kind] + (by_x + by_y,), BF16)
    one, two = ((4, 4, 16), (4, 16)) if kind == "f" else ((4, 64), (64,))
    for axis, width in (("x", by_x), ("y", by_y)):
        HELD["r1" + axis + kind] = ((3,) + one + (width,), BF16)
        HELD["r2" + axis + kind] = ((3,) + two + (width,), BF16)
INPUTS = dict(
    x=((128, 1024), BF16),
    g=((128, 1024), BF16),
    wq=((8, 1024), BF16),
    wk=((8, 1024), BF16),
    wv=((8, 1024), BF16),
    wo8=((8, 1024), BF16),
    wg=((8, 8 * SLICE), BF16),
    wu=((8, 8 * SLICE), BF16),
    extra=((8, 8 * SLICE + 128), F32),
    ids=((8, 1, 256), jnp.int32),
    cosines=((4, 2, 256, 128), F32),
    sines=((4, 2, 256, 128), F32),
)
TABLES = ("cosines", "sines")
FEED = 8 * SLICE
OUTPUTS = dict(
    y=((128, 1024), BF16),
    gx=((128, 1024), F32),
    heads=((4, 64, 1024), BF16),
    feeds=((3, 64, FEED), BF16),
    grad_gains=((64, 128), F32),
)
for given in (INPUTS, OUTPUTS):
    HELD.update({name: spec for name, spec in given.items() if name not in TABLES})
RING, SENDS, LANDINGS, LOCAL = 48, 81, 68, 20


def device(at):
    return (at["xl"] * 4 + at["y"], at["z"] * 4 + at["xh"] * 2 + at["e"])


class Links:
    def __init__(self, send, recv, near):
        self.send, self.recv, self.near = send, recv, near
        self.fixed, self.landings, self.count_near = RING, 0, 0
        self.started = []

    def fixed_slots(self, many):
        self.fixed += many
        return self.fixed - many

    def landing(self, many=1):
        self.landings += many
        return self.landings - many

    def make(self, src, dst, peer, slot, land):
        return pltpu.make_async_remote_copy(
            src_ref=src,
            dst_ref=dst,
            send_sem=self.send.at[slot],
            recv_sem=self.recv.at[land],
            device_id=device(peer),
            device_id_type=MESH,
        )

    def go(self, src, dst, peer, land=None):
        at = len(self.started)
        if at >= RING:
            self.left(at - RING)
        copy = self.make(src, dst, peer, at % RING, self.landing() if land is None else land)
        copy.start()
        self.started.append(copy)
        return copy

    def left(self, at):
        if self.started[at] is not None:
            self.started[at].wait_send()
            self.started[at] = None

    def arrived(self, like, peer, land):
        self.make(like, like, peer, 0, land).wait_recv()

    def here(self, src, dst):
        copy = pltpu.make_async_copy(src, dst, self.near.at[self.count_near])
        self.count_near += 1
        copy.start()
        return copy


def kernel(*refs):
    n_in, n_out = len(INPUTS), len(OUTPUTS)
    given = dict(zip(INPUTS, refs[:n_in]))
    result = dict(zip(OUTPUTS, refs[n_in : n_in + n_out]))
    held = dict(zip(HELD, refs[n_in + n_out : n_in + n_out + len(HELD)]))
    r = types.SimpleNamespace(**held)
    links = Links(*refs[n_in + n_out + len(HELD) :])
    grp, ctx = lax.axis_index("grp"), lax.axis_index("ctx")
    me = {
        "xl": lax.div(grp, 4),
        "y": lax.rem(grp, 4),
        "z": lax.div(ctx, 4),
        "xh": lax.rem(lax.div(ctx, 2), 2),
        "e": lax.rem(ctx, 2),
    }
    xl, y, z, xh, e = (me[k] for k in ("xl", "y", "z", "xh", "e"))
    x = xh * 2 + xl

    def other_core(at):
        return {**at, "e": 1 - at["e"]}

    def along_z(by):
        return {**me, "z": lax.rem(z + by + 4, 4)}

    def in_plane(dx, dy):
        to = lax.rem(x + dx, 4)
        return {**me, "xl": lax.rem(to, 2), "xh": lax.div(to, 2), "y": lax.rem(y + dy, 4)}

    def group(dxl, dy):
        return {**me, "xl": lax.rem(xl + dxl, 2), "y": lax.rem(y + dy, 4)}

    partner = other_core(me)
    across = in_plane(2, 0)
    plane = sorted(
        ((dx, dy) for dx in range(4) for dy in range(4) if dx or dy),
        key=lambda d: -min(d[0], 4 - d[0]) - min(d[1], 4 - d[1]),
    )
    groups = [(dxl, dy) for dxl in range(2) for dy in range(4)]

    came_in = {
        name: links.here(given[name], held[name]) for name in INPUTS if name not in TABLES
    }
    written = []

    def write(name):
        written.append(links.here(held[name], result[name]))

    sem = pltpu.get_barrier_semaphore()

    def greet(peer):
        pl.semaphore_signal(sem, inc=1, device_id=device(peer), device_id_type=MESH)

    row_self = jnp.logical_and(z == y, xl == e)
    head_self = xh == e
    peers = [partner] + [along_z(i) for i in (1, 2, 3)] + [other_core(along_z(i)) for i in (1, 2, 3)]
    peers += [in_plane(*d) for d in plane]
    peers += [other_core(group(0, dy)) for dy in (1, 2, 3)]
    for peer in peers:
        greet(peer)
    for d in groups:
        by_head = {**group(*d), "xh": e, "e": xh}
        by_row = {**me, "xl": e, "y": z, "z": lax.rem(z + d[1], 4), "e": lax.rem(e + d[0], 2)}
        for own, source in ((row_self, by_row), (head_self, by_head)):
            if d != (0, 0):
                greet(source)
            else:
                pl.when(jnp.logical_not(own))(functools.partial(greet, source))
    others = 16 - row_self.astype(jnp.int32) - head_self.astype(jnp.int32)
    tables = [
        links.here(given["cosines"].at[:, xh], r.cos),
        links.here(given["sines"].at[:, xh], r.sin),
    ]
    for copy in came_in.values():
        copy.wait()
    extra = r.extra[...]
    gains = {"attn": extra[:, FEED : FEED + 1], "mlp": extra[:, FEED + 1 : FEED + 2]}
    lane = lax.broadcasted_iota(jnp.int32, (8, WIDE), 1)
    wide = {
        GATE: (r.wg[...].astype(F32) * gains["mlp"], gains["mlp"]),
        GATE + WIDE: (r.wu[...].astype(F32) * gains["mlp"], gains["attn"]),
        DOWN: (extra[:, :FEED], 0.0),
    }
    narrow = [w[...].astype(F32) * gains["attn"] for w in (r.wq, r.wk, r.wv)]
    for s in range(8):
        base = s // 2 * OUT
        for n, whole in enumerate(narrow):
            part = whole[:, s * 128 : (s + 1) * 128]
            r.wsrc[s % 2, :, base + n * 128 : base + (n + 1) * 128] = part
        start, many, rest = window(s)
        for at, (whole, fill) in wide.items():
            part = whole[:, start : start + many]
            if rest:
                part = pltpu.roll(part, many - rest, 1)[:, :WIDE]
            part = jnp.where(lane < SLICE, part, jnp.where(lane == SLICE, fill, 0.0))
            r.wsrc[s % 2, :, base + at : base + at + WIDE] = part
    for h in range(2):
        r.wsrc[h, :, 4 * OUT :] = r.wo8[:, h * 512 : (h + 1) * 512].astype(F32)
    own_rows = pl.ds(pl.multiple_of(e * 8, 8), 8)
    r.pair[own_rows, :] = r.wsrc.at[e][...]

    rows = r.x[...].astype(F32)
    r1 = lax.rsqrt(jnp.mean(rows * rows, axis=-1, keepdims=True) + EPS)
    r.u1.at[z, e][...] = (rows * r1).astype(BF16)
    r.gg.at[z, e][...] = r.g[...]
    pl.semaphore_wait(sem, len(peers) + others)

    class Gather:
        def __init__(self, buf):
            self.buf = buf
            self.land = links.landing(2)

        def start(self):
            mine = self.buf.at[z, e]
            for i in (2, 1, 3):
                links.go(mine, mine, along_z(i), self.land)
            links.go(mine, mine, partner, self.land + 1)

        def pass_on(self):
            links.arrived(self.buf.at[pl.ds(0, 3), 0], partner, self.land)
            for i in (1, 2, 3):
                block = self.buf.at[lax.rem(z + i, 4), e]
                links.go(block, block, partner, self.land + 1)

        def ready(self):
            links.arrived(self.buf.at[:, 0], partner, self.land + 1)

    class QuickGather:
        def __init__(self, buf):
            self.buf = buf
            self.out = {0: None}
            self.over = {}

        def start(self):
            mine = self.buf.at[z, e]
            for i in (1, 3):
                self.out[i] = links.go(mine, mine, along_z(i))
            self.over[0] = links.go(mine, mine, partner)
            self.land = links.landing()

        def pass_on(self, i):
            block = self.buf.at[lax.rem(z - i + 4, 4), e]
            if i == 2:
                links.arrived(block, partner, self.land)
            else:
                self.out[i].wait_recv()
                half = block.at[pl.ds(0 if i == 1 else 64, 64)]
                links.go(half, half, along_z(i), self.land)
            self.over[i] = links.go(block, block, partner)

        def ready(self, i):
            self.over[i].wait_recv()

    class Scatter:
        def __init__(self, kind):
            self.p, self.d, self.r = (held[kind + k] for k in "pdr")
            self.over = {}
            self.land = links.landing()

        def put(self, i, value):
            zz = lax.rem(z - i + 4, 4)
            self.p.at[zz][...] = value.astype(BF16).reshape(2, 128, 1024)
            self.over[i] = links.go(self.p.at[zz, 1 - e], self.d.at[zz], partner)

        def send(self, i):
            zz = lax.rem(z - i + 4, 4)
            if i:
                self.over[i].wait_recv()
                mine = self.p.at[zz, e]
                mine[...] = (mine[...].astype(F32) + self.d.at[zz][...].astype(F32)).astype(BF16)
                links.go(mine, self.r.at[i - 1], along_z(-i), self.land)

        def tile(self, zz, value):
            self.p[zz] = value.astype(BF16).reshape(2, 128, 1024)
            self.over[zz] = links.go(self.p.at[zz, 1 - e], self.d.at[zz], partner)

        def tile_copy(self, zz):
            by = lax.rem(z - zz + 4, 4)
            there = self.r.at[jnp.maximum(by - 1, 0)]
            return links.make(
                self.p.at[zz, e], there, {**me, "z": zz}, self.slots + zz, self.land
            )

        def tile_send(self, zz):
            self.over[zz].wait_recv()

            def away():
                mine = self.p.at[zz, e]
                mine[...] = (mine[...].astype(F32) + self.d[zz].astype(F32)).astype(BF16)
                self.tile_copy(zz).start()

            pl.when(z != zz)(away)

        def total(self, waited=False):
            if not waited:
                self.over[0].wait_recv()
            result = self.p.at[z, e][...].astype(F32) + self.d.at[z][...].astype(F32)
            links.arrived(self.r, partner, self.land)
            for i in range(3):
                result = result + self.r[i].astype(F32)
            return result

    class Spread:
        def __init__(self, buf, along_x, along_y):
            self.own = [buf.at[xl, y, :, xh, :, along_x], buf.at[xl, y, :, xh, :, along_y]]
            self.line = [buf.at[:, y, :, :, :, along_x], buf.at[xl, :, :, xh, :, along_y]]
            three, both = pl.ds(0, 3), (along_x, along_y)
            self.three_own = [buf.at[0, three, :, 0, :, cols] for cols in both]
            self.three_lines = [buf.at[:, three, :, :, :, cols] for cols in both]
            self.land = links.landing(4)

        def start(self):
            for d in (2, 1, 3):
                links.go(self.own[0], self.own[0], in_plane(d, 0), self.land)
                links.go(self.own[1], self.own[1], in_plane(0, d), self.land + 1)

        def pass_on(self, k):
            links.arrived(self.three_own[k], partner, self.land + k)
            for d in (2, 1, 3):
                to = in_plane(d, 0) if k else in_plane(0, d)
                links.go(self.line[k], self.line[k], to, self.land + 2 + k)

        def wait(self):
            for k in range(2):
                links.arrived(self.three_lines[k], partner, self.land + 2 + k)

    class PlaneSum:
        def __init__(self, kind):
            self.by_x = pl.ds(0, SPLIT[kind][0])
            self.by_y = pl.ds(*SPLIT[kind])
            self.g = held["g" + kind]
            self.one = held["r1x" + kind], held["r1y" + kind]
            self.two = held["r2x" + kind], held["r2y" + kind]
            self.feed = kind == "f"
            self.land = links.landing(4)

        def part(self, at_x, at_y, cols):
            if self.feed:
                return self.g.at[:, at_x, at_y, :, cols]
            return self.g.at[at_y, at_x, :, cols]

        def start(self):
            every = slice(None)
            for d in (2, 1, 3):
                there = self.part(lax.rem(x + d, 4), every, self.by_x)
                links.go(there, self.one[0].at[d - 1], in_plane(d, 0), self.land)
                there = self.part(every, lax.rem(y + d, 4), self.by_y)
                links.go(there, self.one[1].at[d - 1], in_plane(0, d), self.land + 1)

        def add(self, mine, landed):
            result = mine[...].astype(F32)
            for d in range(3):
                result = result + landed[d].astype(F32)
            return result

        def middle(self):
            every = slice(None)
            for k in range(2):
                links.arrived(self.one[k], partner, self.land + k)
            mine = self.part(x, every, self.by_x)
            mine[...] = self.add(mine, self.one[0]).astype(BF16)
            mine = self.part(every, y, self.by_y)
            mine[...] = self.add(mine, self.one[1]).astype(BF16)
            for d in (2, 1, 3):
                there = self.part(x, lax.rem(y + d, 4), self.by_x)
                links.go(there, self.two[0].at[d - 1], in_plane(0, d), self.land + 2)
                there = self.part(lax.rem(x + d, 4), y, self.by_y)
                links.go(there, self.two[1].at[d - 1], in_plane(d, 0), self.land + 3)

        def last(self):
            for k in range(2):
                links.arrived(self.two[k], partner, self.land + 2 + k)
            return [
                self.add(self.part(x, y, cols), landed)
                for cols, landed in zip((self.by_x, self.by_y), self.two)
            ]

    class StagedOut:
        def __init__(self, src, dst, relay):
            self.src, self.dst, self.relay = src, dst, relay
            self.slot = y * 2 + e
            self.land = links.landing(2)
            self.fixed = links.fixed_slots(1)
            self.near = links.near.at[links.count_near]
            links.count_near += 1

        def along_y(self, src, at_e):
            mine = self.dst.at[self.slot]
            for dy in (2, 1, 3):
                links.go(src, mine, {**group(0, dy), "e": at_e}, self.land + 1)
            near = pltpu.make_async_copy(src, mine, self.near)
            over = links.make(src, mine, partner, self.fixed, self.land + 1)
            pl.when(e == at_e)(near.start)
            pl.when(e != at_e)(over.start)
            return near, over

        def start(self):
            links.go(self.src, self.relay, group(1, 0), self.land)
            self.along_y(self.src, xl)

        def pass_on(self):
            links.arrived(self.relay, partner, self.land)
            self.local = self.along_y(self.relay, 1 - xl)

        def finish(self):
            near, over = self.local
            near.wait()
            over.wait_send()
            links.arrived(self.dst.at[pl.ds(0, 7)], partner, self.land + 1)

    def hand_out(src, dst, slot, self_is, place):
        first, land = links.fixed_slots(8), links.landing()
        mine = dst.at[slot]
        copies = [
            links.make(src, mine, place(group(*d)), first + n, land)
            for n, d in enumerate(groups)
        ]
        near = pltpu.make_async_copy(src, mine, links.near.at[links.count_near])
        links.count_near += 1
        for copy in copies[1:]:
            copy.start()
        pl.when(self_is)(near.start)
        pl.when(jnp.logical_not(self_is))(copies[0].start)

        def finish():
            def with_own():
                near.wait()
                links.arrived(dst.at[pl.ds(0, 7)], partner, land)

            def without():
                copies[0].wait_send()
                links.arrived(dst, partner, land)

            pl.when(self_is)(with_own)
            pl.when(jnp.logical_not(self_is))(without)
            for copy in copies[1:]:
                copy.wait_send()

        return finish

    swap = links.go(r.wsrc.at[1 - e], r.pair.at[own_rows, :], partner)
    swap.wait_recv()
    for zz in range(4):
        r.wz[zz, :, :OUT] = r.pair[:, zz * OUT : (zz + 1) * OUT].astype(BF16)
        r.wz[zz, :, OUT:] = r.pair[:, 4 * OUT :].astype(BF16)
    land = links.landing()
    for i in (2, 1, 3):
        links.go(r.wz.at[lax.rem(z + i, 4)], r.wrow.at[z], along_z(i), land)
    gather1 = Gather(r.u1)
    gather1.start()
    r.wrow.at[z][...] = r.wz.at[z][...]
    links.arrived(r.wrow.at[pl.ds(0, 3)], partner, land)
    r.w.at[xl, y, :, xh][...] = r.wrow[:, :, :OUT]
    r.wo.at[e, xl, y, :, xh][...] = r.wrow[:, :, OUT:]
    spread_qkv = Spread(r.w, pl.ds(QKV, 128), pl.ds(QKV + 128, 256))
    spread_out = Spread(r.wo.at[e], pl.ds(0, 384), pl.ds(384, 128))
    spread_feed = Spread(r.w, pl.ds(GATE, 768), pl.ds(GATE + 768, 384))
    for spread in (spread_qkv, spread_out, spread_feed):
        spread.start()
    spread_qkv.pass_on(0)
    spread_qkv.pass_on(1)
    gather1.pass_on()
    spread_out.pass_on(0)
    spread_feed.pass_on(0)
    gather_g = Gather(r.gg)
    gather_g.start()
    for copy in tables:
        copy.wait()
    gather1.ready()
    spread_qkv.wait()

    w_qkv = r.w[:, :, :, :, :, QKV:GATE].reshape(1024, GATE - QKV)
    came_kv = []
    for zz in range(4):
        qkv = mm(r.u1[zz].reshape(256, 1024), w_qkv)
        cosine, sine = r.cos[zz], r.sin[zz]
        r.kv.at[zz, xh, 0][...] = turn(qkv[:, 128:256], cosine, sine).astype(BF16)
        r.kv.at[zz, xh, 1][...] = qkv[:, 256:].astype(BF16)
        tile = r.kv.at[zz, xh]
        came_kv.append(links.go(tile, tile, across))
        r.q[zz] = (turn(qkv[:, :128], cosine, sine).astype(BF16) * 0.125).astype(BF16)

    first = lax.broadcasted_iota(jnp.int32, (256, 128), 1) < HD

    def halves(pair):
        zero = jnp.zeros_like(pair)
        return jnp.where(first, pair, zero), jnp.where(first, zero, pair)

    def ids_of(row):
        row = row.astype(F32)
        return row, jnp.broadcast_to(row, (128, row.shape[1])).T[:, :1]

    def pair_ids(p):
        return jnp.concatenate([r.ids[2 * p], r.ids[2 * p + 1]], axis=1)

    def key_tiles(qi, body):
        def whole(p, _):
            body(p, 2, False)
            return 0

        if qi:
            lax.fori_loop(0, qi, whole, 0)
        body(qi, 2, True)
        if qi < 3:
            pl.when(xh == 1)(lambda: body(qi + 1, 1, True))

    mix_slots, mix_land = links.fixed_slots(8), links.landing(2)

    def mix_copy(qi, far):
        at_e = 1 - e if far else e
        to = {**me, "z": qi, "e": at_e}
        src = r.mixb.at[qi, at_e]
        return links.make(
            src, r.mixin.at[z, e], to, mix_slots + 2 * qi + far, mix_land + far
        )

    def attend(qi):
        queries = halves(r.q[qi])
        _, query_ids = ids_of(r.ids.at[2 * qi + xh][...])
        r.top[...] = jnp.full((2, 256, 128), -3e38, F32)

        def one(p, tiles, masked):
            wide = 256 * tiles
            keys = r.kv.at[p, pl.ds(0, tiles), 0][...].reshape(wide, 128)
            for h in range(2):
                score = mt(queries[h], keys)
                if masked:
                    seen = pair_ids(p)[:, :wide].astype(F32) <= query_ids
                    score = jnp.where(seen, score, -1e30)
                r.score.at[h, p, :, pl.ds(0, wide)][...] = score
                top = r.top[h]
                for k in range(wide // 128):
                    top = jnp.maximum(top, score[:, k * 128 : (k + 1) * 128])
                r.top[h] = top

        key_tiles(qi, one)
        tops = [jnp.max(r.top[h], axis=1, keepdims=True) for h in range(2)]
        r.top[...] = jnp.zeros((2, 256, 128), F32)
        r.acc[...] = jnp.zeros((2, 256, 128), F32)

        def two(p, tiles, masked):
            wide = 256 * tiles
            values = r.kv.at[p, pl.ds(0, tiles), 1][...].reshape(wide, 128)
            for h in range(2):
                weight = jnp.exp(r.score.at[h, p, :, pl.ds(0, wide)][...] - tops[h])
                total = r.top[h]
                for k in range(wide // 128):
                    total = total + weight[:, k * 128 : (k + 1) * 128]
                r.top[h] = total
                r.acc[h] += mm(weight.astype(BF16), values)

        key_tiles(qi, two)
        sums = [jnp.sum(r.top[h], axis=1, keepdims=True) for h in range(2)]
        mixed = jnp.where(first, r.acc[0] / sums[0], r.acc[1] / sums[1])
        r.mix.at[qi][...] = mixed
        r.lse.at[qi][...] = jnp.where(
            first, tops[0] + jnp.log(sums[0]), tops[1] + jnp.log(sums[1])
        )
        r.mixb.at[qi][...] = mixed.astype(BF16).reshape(2, 128, 128)
        mix_copy(qi, 1).start()
        pl.when(z != qi)(lambda: mix_copy(qi, 0).start())


    def turn_units(b, _):
        cols = pl.ds(pl.multiple_of(b * 256, 256), 256)
        r.u1t[cols, :] = r.u1[:, :, :, cols].reshape(1024, 256).T
        return 0

    lax.fori_loop(0, 4, turn_units, 0)
    came_kv[0].wait_recv()
    for qi in range(4):
        if qi < 3:
            came_kv[qi + 1].wait_recv()
        if qi == 2:
            spread_out.pass_on(1)
            spread_feed.pass_on(1)
        attend(qi)
        if qi == 1:
            gather_g.pass_on()
    r.mixin.at[z, e][...] = r.mixb.at[z, e][...]

    spread_out.wait()
    half = links.go(r.wo.at[e], r.wo.at[e], partner)
    links.arrived(r.mixin.at[pl.ds(0, 3), 0], partner, mix_land)
    links.arrived(r.mixin.at[:, 0], partner, mix_land + 1)
    half.wait_recv()
    mixed = jnp.concatenate([r.mixin[s // 2, s % 2] for s in range(8)], axis=1)
    hidden = r.x[...].astype(F32) + jnp.concatenate(
        [mm(mixed, r.wo[h].reshape(1024, 512)) for h in range(2)], axis=1
    )
    r2 = lax.rsqrt(jnp.mean(hidden * hidden, axis=-1, keepdims=True) + EPS)
    unit2 = hidden * r2
    r.hidden[...] = hidden
    r.unit2[...] = unit2
    r.r2[...] = r2
    r.u2.at[z, e][...] = unit2.astype(BF16)
    gather2 = QuickGather(r.u2)
    gather2.start()
    spread_feed.wait()
    gather_g.ready()
    w_down = r.w[:, :, :, :, :, DOWN:OUT].reshape(1024, WIDE)

    def down_back(zz, _):
        back = mm(r.gg.at[zz][...].reshape(256, 1024), w_down)
        r.score.at[0, zz, :, :WIDE][...] = back
        return 0

    lax.fori_loop(0, 4, down_back, 0)

    w_up = r.w[:, :, :, :, :, GATE:DOWN].reshape(1024, 2 * WIDE)
    real = lax.broadcasted_iota(jnp.int32, (256, WIDE), 1) < SLICE
    scatter2, scatter_y = Scatter("e2"), Scatter("out")
    for at, i in enumerate(NEAR):
        if at == 1:
            gather2.pass_on(1)
            gather2.pass_on(3)
        if at == 3:
            gather2.pass_on(2)
        gather2.ready(i)
        zz = lax.rem(z - i + 4, 4)
        sums = mm(r.u2.at[zz][...].reshape(256, 1024), w_up)
        gate, up = sums[:, :WIDE], sums[:, WIDE:]
        sigmoid = 1.0 / (1.0 + jnp.exp(-gate))
        swish = gate * sigmoid
        back = r.score.at[0, zz, :, :WIDE][...]
        act = jnp.where(real, swish * up, 0.0).astype(BF16)
        r.act.at[pl.ds(4 * zz, 4)][...] = act.reshape(4, 64, WIDE)
        d_gate = back * up * sigmoid * (1.0 + gate * (1.0 - sigmoid))
        d_gate = jnp.where(real, d_gate, 0.0).astype(BF16)
        d_up = jnp.where(real, back * swish, 0.0).astype(BF16)
        r.dgu.at[zz][...] = jnp.concatenate([d_gate, d_up], axis=1)
        scatter2.put(i, mt(r.dgu.at[zz][...], w_up))
        if at:
            scatter2.send(NEAR[at - 1])
    scatter2.send(NEAR[3])

    gain_lane = SLICE

    def feed_grads(b, _):
        cols = pl.ds(pl.multiple_of(b * 256, 256), 256)
        units = r.u2[:, :, :, cols].reshape(1024, 256)
        grads = tm(units, r.dgu[...].reshape(1024, 2 * WIDE))
        weights = r.w.at[lax.div(b, 2), pl.ds(2 * lax.rem(b, 2), 2), :, :, :, GATE:DOWN]
        weights = weights[...].reshape(256, 2 * WIDE).astype(F32)
        gain = weights[:, gain_lane : gain_lane + 1]
        lane = lax.broadcasted_iota(jnp.int32, (256, 2 * WIDE), 1)
        keep = lax.rem(lane, WIDE) < SLICE
        weighed = jnp.sum(jnp.where(keep, weights * grads, 0.0), axis=1, keepdims=True) / gain
        shape = (4, 4, 16, -1)
        r.gf.at[b, :, :, :, : 2 * WIDE][...] = (grads * gain).astype(BF16).reshape(shape)
        downs = tm(
            r.gg[:, :, :, cols].reshape(1024, 256), r.act[...].reshape(1024, WIDE)
        )
        lane = lax.broadcasted_iota(jnp.int32, (256, WIDE), 1)
        downs = jnp.where(lane == gain_lane, weighed, downs)
        r.gf.at[b, :, :, :, 2 * WIDE :][...] = downs.astype(BF16).reshape(shape)
        return 0

    lax.fori_loop(0, 4, feed_grads, 0)
    sum_f = PlaneSum("f")
    sum_f.start()

    def down_out(i):
        zz = lax.rem(z - i + 4, 4)
        scatter_y.put(i, mt(r.act.at[pl.ds(4 * zz, 4)][...].reshape(256, WIDE), w_down))

    e2 = scatter2.total()
    unit2 = r.unit2[...]
    grad_hidden = r.g[...].astype(F32) + r.r2[...] * (
        e2 - unit2 * jnp.mean(e2 * unit2, axis=-1, keepdims=True)
    )
    r.gh[...] = grad_hidden
    branch = grad_hidden.astype(BF16)
    r.db.at[z, e][...] = branch
    d_mixed = mt(branch[:, :512], r.wo[0].reshape(1024, 512)) + mt(
        branch[:, 512:], r.wo[1].reshape(1024, 512)
    )
    for s in range(8):
        r.dmixb[s // 2, s % 2] = d_mixed[:, s * 128 : (s + 1) * 128].astype(BF16)
    came_mix = links.landing()
    for i in NEAR:
        to = along_z(i)
        for to_e, peer in ((1 - e, other_core(to)), (e, to)):
            if i or peer is not to:
                src = r.dmixb.at[to["z"], to_e]
                links.go(src, r.dmix.at[z, e], peer, came_mix)
    r.dmix.at[z, e][...] = r.dmixb.at[z, e][...]

    gather_b = Gather(r.db)
    gather_b.start()
    for at, i in enumerate(NEAR):
        down_out(i)

    def out_grads():
        grads = tm(r.mixb[...].reshape(1024, 128), r.db[...].reshape(1024, 1024))
        grads = grads.astype(BF16)
        for j in range(2):
            for k in range(8):
                r.go[j, k] = grads[j * 64 : (j + 1) * 64, k * 128 : (k + 1) * 128]
        land = links.landing()
        for n, d in enumerate(plane):
            to = in_plane(*d)
            src = r.go.at[to["xh"], to["xl"] * 4 + to["y"]]
            links.go(src, r.gor.at[n], to, land)
        return land

    for p in range(4):
        r.kt[p] = r.kv[p, :, 0].reshape(512, 128).T

    links.arrived(r.gor.at[pl.ds(0, 14)], partner, came_mix)
    r.dkv[...] = jnp.zeros((4, 2, 256, 256), F32)
    dkv_slots, dkv_land = links.fixed_slots(4), links.landing(4)

    def dkv_copy(zz):
        return links.make(
            r.dkvs.at[zz], r.dkvr.at[zz], across, dkv_slots + zz, dkv_land + zz
        )

    def give(zz):
        both = r.dkv.at[zz, 1 - xh][...].astype(BF16)
        r.dkvs.at[zz, 0][...] = both[:, :128]
        r.dkvs.at[zz, 1][...] = both[:, 128:]
        dkv_copy(zz).start()

    def attend_back(qi):
        queries = halves(r.q[qi])
        grads = r.dmix[qi].reshape(256, 128)
        product = (grads.astype(F32) * r.mix[qi]).T
        grads = halves(grads)
        dots = [jnp.sum(product[k : k + HD], axis=0, keepdims=True) for k in (0, HD)]
        logs = r.lse[qi].T
        logs = [logs[k : k + 1] for k in (0, HD)]
        query_ids = r.ids.at[2 * qi + xh][...].astype(F32)
        def one(p, tiles, masked):
            wide = 256 * tiles
            keys, values = (
                r.kv.at[p, pl.ds(0, tiles), k][...].reshape(wide, 128) for k in range(2)
            )
            keys_turned = r.kt.at[p, :, pl.ds(0, wide)][...]
            d_key, d_value = 0.0, 0.0
            for h in range(2):
                score = mt(keys, queries[h])
                if masked:
                    _, key_ids = ids_of(pair_ids(p)[:, :wide])
                    score = jnp.where(key_ids <= query_ids, score, -1e30)
                prob = jnp.exp(score - logs[h])
                d_score = (prob * (mt(values, grads[h]) - dots[h])).astype(BF16)
                d_value += mm(prob.astype(BF16), grads[h])
                d_key += mm(d_score, queries[h])
                r.dqt[h * HD : (h + 1) * HD] += mm(
                    keys_turned[h * HD : (h + 1) * HD], d_score
                )
            both = jnp.concatenate([d_key, d_value], axis=1).reshape(tiles, 256, 256)
            r.dkv.at[p, pl.ds(0, tiles)][...] += both

        r.dqt[...] = jnp.zeros((128, 256), F32)
        key_tiles(qi, one)
        r.dq[qi] = (r.dqt[...] * 0.125).T
        if qi < 3:
            give(qi + 1)

    attend_back(3)
    for i in NEAR[1:]:
        scatter_y.send(i)
    sum_f.middle()
    attend_back(2)
    r.sf[...] = jnp.concatenate(sum_f.last(), axis=-1).astype(BF16)
    land_sf = links.landing()
    for i in (2, 1, 3):
        to = along_z(i)
        links.go(r.sf.at[to["z"]], r.zf.at[z], to, land_sf)
    r.zf.at[z][...] = r.sf.at[z][...]
    gather_b.pass_on()
    attend_back(1)
    gather_b.ready()
    sum_o = out_grads()
    attend_back(0)
    give(0)
    links.arrived(r.zf.at[pl.ds(0, 3)], partner, land_sf)
    out_f = StagedOut(r.zf, r.ff, r.relay)
    out_f.start()

    scatter1 = Scatter("e1")
    scatter1.slots = links.fixed_slots(4)
    for zz in (3, 2, 1, 0):
        dkv_copy(zz).wait_recv()
        cosine, sine = r.cos[zz], -r.sin[zz]
        d_tile = r.dkv.at[zz, xh][...]
        d_key = d_tile[:, :128] + r.dkvr[zz, 0].astype(F32)
        d_value = d_tile[:, 128:] + r.dkvr[zz, 1].astype(F32)
        r.dqkv[zz] = jnp.concatenate(
            [
                turn(r.dq[zz], cosine, sine).astype(BF16),
                turn(d_key, cosine, sine).astype(BF16),
                d_value.astype(BF16),
            ],
            axis=1,
        )

    def attn_gains(rows):
        at = GATE + WIDE + 256
        last = rows[..., at : at + 128]
        return last.reshape(-1, 128).astype(F32)[:, gain_lane - 256 : gain_lane - 255]

    def qkv_grads(b, _):
        cols = pl.ds(pl.multiple_of(b * 256, 256), 256)
        grads = mm(r.u1t[cols, :], r.dqkv[...].reshape(1024, 384))
        rows = r.w.at[lax.div(b, 2), pl.ds(2 * lax.rem(b, 2), 2)]
        r.gq.at[b][...] = (grads * attn_gains(rows)).astype(BF16).reshape(4, 64, 384)
        return 0

    lax.fori_loop(0, 4, qkv_grads, 0)
    sum_q = PlaneSum("q")
    sum_q.start()
    for zz in (3, 2, 1, 0):
        scatter1.tile(zz, mt(r.dqkv[zz], w_qkv))
        if zz < 3:
            scatter1.tile_send(zz + 1)
    scatter1.tile_send(0)
    out_f.pass_on()
    sum_q.middle()
    r.y[...] = (r.hidden[...] + scatter_y.total()).astype(BF16)
    write("y")

    total = r.go.at[xh, grp][...].astype(F32)
    links.arrived(r.gor, partner, sum_o)
    for n in range(15):
        total = total + r.gor[n].astype(F32)
    r.so[...] = total.astype(BF16)
    done_o = hand_out(r.so, r.fo, grp, head_self, lambda at: {**at, "xh": e, "e": xh})
    summed = jnp.concatenate(sum_q.last(), axis=-1)
    block = 4 * y + x
    rows = r.w.at[lax.div(block, 8), lax.rem(lax.div(block, 2), 4), pl.ds(2 * lax.rem(block, 2), 2)]
    gain = attn_gains(rows)
    weights = rows[:, :, :, :GATE].reshape(64, GATE).astype(F32)
    weighed = jnp.sum(weights * summed, axis=1, keepdims=True) / (gain * gain)
    r.sq[:, :GATE] = summed.astype(BF16)
    r.sq[:, GATE:] = jnp.broadcast_to(weighed, (64, 128)).astype(BF16)
    done_q = hand_out(r.sq, r.fq, z * 2 + e, row_self, lambda at: {**at, "z": y, "e": xl})
    e1 = scatter1.total(True)
    rows = r.x[...].astype(F32)
    r1 = lax.rsqrt(jnp.mean(rows * rows, axis=-1, keepdims=True) + EPS)
    unit1 = rows * r1
    r.gx[...] = r.gh[...] + r1 * (
        e1 - unit1 * jnp.mean(e1 * unit1, axis=-1, keepdims=True)
    )
    write("gx")

    def rows_of(landed, s):
        pieces = [landed[2 * k + s % 2, s // 2] for k in range(4)]
        return jnp.concatenate(pieces, axis=0).astype(F32)

    out_f.finish()
    r.feeds[...] = jnp.zeros((3, 64, FEED), BF16)
    lane = lax.broadcasted_iota(jnp.int32, (64, WIDE), 1)
    for s in range(8):
        part = rows_of(r.ff, s)
        start, many, rest = window(s)
        for n in range(3):
            piece = jnp.where(lane < SLICE, part[:, n * WIDE : (n + 1) * WIDE], 0.0)
            if many > WIDE:
                piece = jnp.concatenate([piece, jnp.zeros((64, 128), F32)], axis=1)
            if rest:
                piece = pltpu.roll(piece, rest, 1)
            r.feeds[n, :, start : start + many] += piece.astype(BF16)
        weighed = part[:, 2 * WIDE + SLICE : 2 * WIDE + SLICE + 1]
        gain_mlp = weighed + (gain_mlp if s else 0.0)
    write("feeds")
    done_o()
    for k in range(8):
        r.heads[3, :, k * 128 : (k + 1) * 128] = r.fo[k]
    done_q()
    for s in range(8):
        part = r.fq[s].astype(F32)
        for n in range(3):
            piece = part[:, n * 128 : (n + 1) * 128]
            r.heads[n, :, s * 128 : (s + 1) * 128] = piece.astype(BF16)
        gain_attn = part[:, 384:] + (gain_attn if s else 0.0)
    lane = lax.broadcasted_iota(jnp.int32, (64, 128), 1)
    r.grad_gains[...] = jnp.where(lane == 0, gain_attn, gain_mlp)
    write("heads")
    write("grad_gains")
    for zz in range(4):
        mix_copy(zz, 1).wait_send()
        pl.when(z != zz)(lambda: mix_copy(zz, 0).wait_send())
        dkv_copy(zz).wait_send()
        pl.when(z != zz)(lambda: scatter1.tile_copy(zz).wait_send())
    for at in range(len(links.started) - RING, len(links.started)):
        links.left(at)
    for copy in written:
        copy.wait()
    counts = links.fixed, links.landings, links.count_near
    assert counts == (SENDS, LANDINGS, LOCAL), counts


def rope_tables():
    positions = np.arange(2048, dtype=np.float32)[:, None]
    frequency = np.float32(10000.0) ** (
        np.float32(-2.0) * np.arange(32, dtype=np.float32) / np.float32(64)
    )
    angles = positions * frequency.astype(np.float32)[None, :]
    cosine, sine = np.cos(angles), np.sin(angles)
    cosines = np.concatenate([cosine] * 4, axis=1)
    sines = np.concatenate([-sine, sine, -sine, sine], axis=1)
    shape = (4, 2, 256, 128)
    return cosines.astype(np.float32).reshape(shape), sines.astype(np.float32).reshape(shape)


def per_device(
    tokens,
    blocks,
    w_query,
    w_key,
    w_value,
    w_out,
    w_gate,
    w_up,
    w_down,
    norm_attn,
    norm_mlp,
    cotangent,
):
    gains = jnp.stack([norm_attn, norm_mlp], axis=1)
    extra = jnp.concatenate([w_down.T, jnp.pad(gains, ((0, 0), (0, 126)))], axis=1).astype(F32)
    cosines, sines = rope_tables()
    anywhere = pl.BlockSpec(memory_space=pl.ANY)
    y, gx, heads, feeds, gains = pl.pallas_call(
        kernel,
        out_shape=[jax.ShapeDtypeStruct(*spec) for spec in OUTPUTS.values()],
        in_specs=[anywhere] * len(INPUTS),
        out_specs=[anywhere] * len(OUTPUTS),
        scratch_shapes=[pltpu.VMEM(*spec) for spec in HELD.values()]
        + [
            pltpu.SemaphoreType.DMA((SENDS,)),
            pltpu.SemaphoreType.DMA((LANDINGS,)),
            pltpu.SemaphoreType.DMA((LOCAL,)),
        ],
        compiler_params=pltpu.CompilerParams(
            collective_id=0, has_side_effects=True, vmem_limit_bytes=63 * 2**20
        ),
    )(
        tokens[0],
        cotangent[0],
        w_query,
        w_key,
        w_value,
        w_out,
        w_gate,
        w_up,
        extra,
        blocks.reshape(8, 1, 256),
        jnp.asarray(cosines),
        jnp.asarray(sines),
    )

    return (
        y[None],
        gx[None],
        *[heads[n].astype(F32) for n in range(4)],
        feeds[0].astype(F32),
        feeds[1].astype(F32),
        feeds[2].astype(F32).T,
        gains[:, 0],
        gains[:, 1],
    )


def solution(mesh):
    both = ("grp", "ctx")
    row = P(both, None)
    tokens = P("grp", "ctx", None)
    shard = P("ctx", None)
    return jax.shard_map(
        per_device,
        mesh=mesh,
        in_specs=(
            tokens,
            P("grp", None),
            *[row] * 6,
            P(None, both),
            P(both),
            P(both),
            tokens,
        ),
        out_specs=(tokens, tokens, *[shard] * 6, P(None, "ctx"), P("ctx"), P("ctx")),
        check_vma=False,
    )
```

profile of v0, /device:TPU:0, one launch (start us, length us, event | category | flops | bytes accessed | tf_op | source)
XLA Modules:
  0.0 155.3 jit_solution(9047214001343571731)
XLA Ops:
  0.6 0.7 pad_maximum_fusion
  1.3 0.1 copy.29
  1.4 1.4 fusion.2.refs_8_
  2.9 145.9 %shard_map.221 = (bf16[128,1024]{1,0:T(8,128)(2,1)}, f32[128,1024]{1,0:T(8,128)}, bf16[4,64,1024]{2,1,0:T(8,128)(2,1)}, bf16[3,64,2816]{2,1,0:T(8,128)(2,1)}, f32[64,128]{1,0:T(8,128)}) custom-call(bf16[128,1024]{1,0:T(8,128)(2,1)} %bitcast.33, bf16[128,1024]{1,0:T(8,128)(2,1)} %bitcast.34, bf16[8,1024]{1,0:T(8,128)(2,1)} %refs_2_.1, ...), custom_call_target="tpu_custom_call" | custom-call | tf_op jit(solution)/shard_map/pallas_call | solution.py:1013
  148.8 0.0 copy-start
  148.8 1.6 %slice_reduce_fusion = (f32[64]{0:T(128)}, f32[64]{0:T(128)}) fusion(f32[64,128]{1,0:T(8,128)} %get-tuple-element.20), kind=kLoop, calls=%fused_computation.11 | loop fusion | bytes 1024 | tf_op jit(solution)/shard_map/slice | solution.py:1050
  150.3 2.1 %bitcast_convert_fusion.2 = (f32[64,1024]{1,0:T(8,128)}, f32[64,1024]{1,0:T(8,128)}, f32[64,1024]{1,0:T(8,128)}, f32[64,1024]{1,0:T(8,128)}) fusion(bf16[4,64,1024]{2,1,0:T(8,128)(2,1)} %get-tuple-element.18), kind=kLoop, calls=%fused_computation.3 | loop fusion | flops 262144 | bytes 1572864 | tf_op jit(solution)/shard_map/convert_element_type | solution.py:1045
  152.4 0.0 copy-done
  152.4 0.0 copy-start.2
  152.4 0.0 copy-start.1
  152.4 1.4 convert_bitcast_fusion
  153.8 0.0 copy-done.2
  153.8 0.7 copy.32
  154.5 0.0 copy-done.1
  154.5 0.8 copy.33
Async XLA Ops:
  148.8 3.7 %copy-start = (bf16[3,64,2816]{2,1,0:T(8,128)(2,1)S(1)}, bf16[3,64,2816]{2,1,0:T(8,128)(2,1)}, u32[]{:S(2)}) copy-start(bf16[3,64,2816]{2,1,0:T(8,128)(2,1)} %get-tuple-element.19) | copy-start | bytes 3244036
  152.4 1.4 copy-start.2
  152.4 2.1 %copy-start.1 = (f32[128,1024]{1,0:T(8,128)S(1)}, f32[128,1024]{1,0:T(8,128)}, u32[]{:S(2)}) copy-start(f32[128,1024]{1,0:T(8,128)} %get-tuple-element.17) | copy-start | bytes 1572868
where the time goes:
time: 156 us; the launch traced here: 155 us
  Pallas kernels  146 us (94%)
  other arithmetic  5.58 us (4%)
  local copies, waits for them, and re-layouts  3.17 us (2%)
    pallas_call x1, Pallas kernels, per_device(): pl.pallas_call(kernel, out_shape=[jax.ShapeDtypeStruct(*spec) for spec in...  146 us

commit v1 on v0

--- a/solution.py
+++ b/solution.py
@@ -126,7 +126,7 @@
     gx=((128, 1024), F32),
     heads=((4, 64, 1024), BF16),
     feeds=((3, 64, FEED), BF16),
-    grad_gains=((64, 128), F32),
+    grad_gains=((8, 128), F32),
 )
 for given in (INPUTS, OUTPUTS):
     HELD.update({name: spec for name, spec in given.items() if name not in TABLES})
@@ -657,8 +657,9 @@
     for qi in range(4):
         if qi < 3:
             came_kv[qi + 1].wait_recv()
+        if qi == 1:
+            spread_out.pass_on(1)
         if qi == 2:
-            spread_out.pass_on(1)
             spread_feed.pass_on(1)
         attend(qi)
         if qi == 1:
@@ -682,8 +683,16 @@
     r.u2.at[z, e][...] = unit2.astype(BF16)
     gather2 = QuickGather(r.u2)
     gather2.start()
+    gather_g.ready()
+
+    def turn_grads(b, _):
+        cols = pl.ds(pl.multiple_of(b * 256, 256), 256)
+        turned = r.gg[:, :, :, cols].reshape(1024, 256).T
+        r.e1p.at[b][...] = turned.reshape(2, 128, 1024)
+        return 0
+
+    lax.fori_loop(0, 4, turn_grads, 0)
     spread_feed.wait()
-    gather_g.ready()
     w_down = r.w[:, :, :, :, :, DOWN:OUT].reshape(1024, WIDE)
 
     def down_back(zz, _):
@@ -734,9 +743,7 @@
         weighed = jnp.sum(jnp.where(keep, weights * grads, 0.0), axis=1, keepdims=True) / gain
         shape = (4, 4, 16, -1)
         r.gf.at[b, :, :, :, : 2 * WIDE][...] = (grads * gain).astype(BF16).reshape(shape)
-        downs = tm(
-            r.gg[:, :, :, cols].reshape(1024, 256), r.act[...].reshape(1024, WIDE)
-        )
+        downs = mm(r.e1p.at[b][...].reshape(256, 1024), r.act[...].reshape(1024, WIDE))
         lane = lax.broadcasted_iota(jnp.int32, (256, WIDE), 1)
         downs = jnp.where(lane == gain_lane, weighed, downs)
         r.gf.at[b, :, :, :, 2 * WIDE :][...] = downs.astype(BF16).reshape(shape)
@@ -963,7 +970,7 @@
             r.heads[n, :, s * 128 : (s + 1) * 128] = piece.astype(BF16)
         gain_attn = part[:, 384:] + (gain_attn if s else 0.0)
     lane = lax.broadcasted_iota(jnp.int32, (64, 128), 1)
-    r.grad_gains[...] = jnp.where(lane == 0, gain_attn, gain_mlp)
+    r.grad_gains[:, :64] = jnp.where(lane == 0, gain_attn, gain_mlp).T[:8]
     write("heads")
     write("grad_gains")
     for zz in range(4):
@@ -1046,8 +1053,8 @@
         feeds[0].astype(F32),
         feeds[1].astype(F32),
         feeds[2].astype(F32).T,
-        gains[:, 0],
-        gains[:, 1],
+        gains[0, :64],
+        gains[1, :64],
     )
 
 

time: 156 us -> 156 us (level)
    slice x1 -> x0, local copies, waits for them, and re-layouts: 1.57 us -> none  [per_device(): gains[:, 1]]
where the time goes in v1:
time: 156 us; the launch traced here: 155 us
  Pallas kernels  146 us (94%)
  other arithmetic  5.58 us (4%)
  local copies, waits for them, and re-layouts  2.9 us (2%)
    pallas_call x1, Pallas kernels, per_device(): pl.pallas_call(kernel, out_shape=[jax.ShapeDtypeStruct(*spec) for spec in...  146 us

profile of v1, /device:TPU:0, one launch (start us, length us, event | category | flops | bytes accessed | tf_op | source)
XLA Modules:
  0.0 154.9 jit_solution(14980611694635785028)
XLA Ops:
  0.6 0.7 pad_maximum_fusion
  1.3 0.1 copy.27
  1.4 1.4 fusion.2.refs_8_
  2.9 145.8 %shard_map.221 = (bf16[128,1024]{1,0:T(8,128)(2,1)}, f32[128,1024]{1,0:T(8,128)}, bf16[4,64,1024]{2,1,0:T(8,128)(2,1)}, bf16[3,64,2816]{2,1,0:T(8,128)(2,1)}, f32[8,128]{1,0:T(8,128)}) custom-call(bf16[128,1024]{1,0:T(8,128)(2,1)} %bitcast.37, bf16[128,1024]{1,0:T(8,128)(2,1)} %bitcast.38, bf16[8,1024]{1,0:T(8,128)(2,1)} %refs_2_.1, ...), custom_call_target="tpu_custom_call" | custom-call | tf_op jit(solution)/shard_map/pallas_call | solution.py:1020
  148.6 0.0 copy-start
  148.6 1.3 slice_bitcast_fusion
  149.9 2.1 %bitcast_convert_fusion.2 = (f32[64,1024]{1,0:T(8,128)}, f32[64,1024]{1,0:T(8,128)}, f32[64,1024]{1,0:T(8,128)}, f32[64,1024]{1,0:T(8,128)}) fusion(bf16[4,64,1024]{2,1,0:T(8,128)(2,1)} %get-tuple-element.18), kind=kLoop, calls=%fused_computation.3 | loop fusion | flops 262144 | bytes 1572864 | tf_op jit(solution)/shard_map/convert_element_type | solution.py:1052
  152.0 0.0 copy-done
  152.0 0.0 copy-start.2
  152.0 0.0 copy-start.1
  152.0 1.4 convert_bitcast_fusion
  153.4 0.0 copy-done.2
  153.4 0.7 copy.30
  154.1 0.0 copy-done.1
  154.1 0.8 copy.31
Async XLA Ops:
  148.6 3.4 %copy-start = (bf16[3,64,2816]{2,1,0:T(8,128)(2,1)S(1)}, bf16[3,64,2816]{2,1,0:T(8,128)(2,1)}, u32[]{:S(2)}) copy-start(bf16[3,64,2816]{2,1,0:T(8,128)(2,1)} %get-tuple-element.19) | copy-start | bytes 3244036
  152.0 1.4 copy-start.2
  152.0 2.1 %copy-start.1 = (f32[128,1024]{1,0:T(8,128)S(1)}, f32[128,1024]{1,0:T(8,128)}, u32[]{:S(2)}) copy-start(f32[128,1024]{1,0:T(8,128)} %get-tuple-element.17) | copy-start | bytes 1572868
